TPU v7x, 512 devices: a whole 4x8x8 slice. The times are simulated.
512 devices in a mesh: blk: 64 (over z, y_hi, x), col: 8 (over y_lo, core).
Axes of the slice: x: 4, y: 8 (y_hi: 2, y_lo: 4; y = y_hi * 4 + y_lo), z: 8, core: 2. Of those that a mesh axis runs over, the one named last changes fastest.
Arguments:
- queries: bfloat16 [512, 16384], P('blk', 'col'), may hold values from -6 to 6
- factor: bfloat16 [16384, 1024], P('col', 'blk'), may hold values from -0.046875 to 0.046875
- eigenvalues: float32 [1024], replicated, may hold values from 0.05 to 20
- damping: float32 [1], replicated, may hold values from 0.5 to 2
- train_rows: bfloat16 [65536, 16384], P('blk', 'col'), may hold values from -0.046875 to 0.046875
Outputs:
- scores: bfloat16 [512, 65536], P('col', 'blk')
All inputs are finite; a program needn't handle non-finite values.
Results may differ from a plain program's by a relative error of at most 0.0049.
Values may be sent and summed in bfloat16 or wider, within the bound.
No kernel may reach another device: no remote copies, remote signals or barrier semaphores. Data moves between devices by JAX's collectives and lax.ppermute only.
A program may use at most 64 MiB of HBM per device.

v0:
```python
import jax
import jax.numpy as jnp
from jax import lax
from jax.sharding import Mesh
from jax.sharding import PartitionSpec as P

BLK = ("blk_0", "blk_1", "blk_2")


def in_order(tiles, dim):
    shape = list(tiles.shape[1:])
    shape[dim] *= tiles.shape[0]
    return jnp.moveaxis(tiles, 0, dim).reshape(shape)


def stacked_from(shard, axes, turns):
    tiles = shard[None]
    for k in turns:
        tiles = lax.all_gather(tiles, axes[k], axis=0, tiled=True)
    carried = [lax.axis_size(axes[k]) for k in reversed(turns)]
    tiles = tiles.reshape(*carried, *shard.shape)
    turned = sorted(range(len(turns)), key=lambda place: turns[len(turns) - 1 - place])
    return tiles.transpose(*turned, *range(len(turns), tiles.ndim)).reshape(-1, *shard.shape)


def gather_axes(shard, axes, turns, dim):
    return in_order(stacked_from(shard, axes, turns), dim)


def from_everyone(shard, axis):
    length = lax.axis_size(axis)
    return lax.all_to_all(
        jnp.broadcast_to(shard[None], (length, *shard.shape)), axis, 0, 0, tiled=True
    )


def taken_together(shard, axis):
    return from_everyone(shard, axis).sum(axis=0)


def row_scores(block_rows, train_rows):
    return jnp.einsum("qk,nk->qn", block_rows, train_rows, preferred_element_type=jnp.float32)


def per_device(queries, factor, eigenvalues, damping, train_rows):
    damp_value = damping[0]
    weights = eigenvalues / (eigenvalues + damp_value)
    full_factor = gather_axes(factor, BLK, (1, 0, 2), 1)
    partial_value = jnp.dot(queries, full_factor, preferred_element_type=jnp.float32)
    coefficient = taken_together(partial_value, "col")
    scaled = coefficient * weights[None, :]
    correction = jnp.dot(scaled, full_factor.astype(jnp.float32).T, precision=lax.Precision.HIGHEST)
    pre_own = ((queries.astype(jnp.float32) - correction) / damp_value).astype(jnp.bfloat16)
    partial_scores = row_scores(lax.all_gather(pre_own, BLK, axis=0, tiled=True), train_rows)
    scores = lax.psum_scatter(partial_scores, "col", scatter_dimension=0, tiled=True)
    return scores.astype(jnp.bfloat16)


def solution(mesh):
    split = Mesh(
        mesh.devices.reshape(8, 2, 4, mesh.shape["col"]), ("blk_0", "blk_1", "blk_2", "col")
    )
    in_specs = (P(BLK, "col"), P("col", BLK), P(), P(), P(BLK, "col"))
    out_specs = P("col", BLK)
    return jax.shard_map(
        per_device, mesh=split, in_specs=in_specs, out_specs=out_specs, check_vma=False
    )
```

profile of v0, /device:TPU:6, one launch (start us, length us, event | category | flops | bytes accessed | tf_op | source)
XLA Modules:
  0.0 330.9 jit_solution(12432319824471753628)
XLA Ops:
  6.5 0.0 all-gather.5.cloned.1.call-start
  6.5 9.7 %all-gather = bf16[4096,16]{0,1:T(8,128)(2,1)S(1)} all-gather(bf16[2048,16]{0,1:T(8,128)(2,1)} %param.6), channel_id=2, replica_groups=mesh['blk_0'=8,'blk_1'=2,'blk_2'=4,'col'=8] {'blk_1'}, dimensions={0}, use_global_device_ids=true | all-gather | bytes 196608 | tf_op jit(solution)/shard_map/all_gather | solution.py:19
  16.2 0.7 copy.17
  16.9 0.0 all-gather.5.cloned.1.call-update
  16.9 0.0 all-gather.7.cloned.1.call-start
  17.0 47.4 %all-gather.5.cloned.1.call-done = bf16[16,2048,16]{1,2,0:T(8,128)(2,1)} async-done(((bf16[2,2048,16]{1,2,0:T(8,128)(2,1)}), bf16[16,2048,16]{1,2,0:T(8,128)(2,1)}) %all-gather.5.cloned.1.call-update) | async-done | bytes 1048592 | tf_op jit(solution)/shard_map/all_gather | solution.py:19
  64.4 0.0 all-gather.7.cloned.1.call-update
  64.4 52.0 %all-gather.7.cloned.1.call-done = bf16[64,2048,16]{1,2,0:T(8,128)(2,1)} async-done(((bf16[16,2048,16]{1,2,0:T(8,128)(2,1)}), bf16[64,2048,16]{1,2,0:T(8,128)(2,1)}) %all-gather.7.cloned.1.call-update) | async-done | bytes 4194320 | tf_op jit(solution)/shard_map/all_gather | solution.py:19
  116.4 0.0 copy-start.1
  116.4 2.5 copy.14
  118.9 0.0 copy-start
  118.9 0.0 copy-start.2
  118.9 1.9 copy-done
  120.9 0.0 copy-done.1
  120.9 1.2 fusion.4
  122.1 0.7 broadcast_in_dim.5
  122.8 4.8 %all-to-all-start = ((f32[8,8,1024]{2,1,0:T(8,128)}), f32[8,8,1024]{2,1,0:T(8,128)S(1)}, u32[]{:S(2)}, u32[]{:S(2)}) async-start(f32[8,8,1024]{2,1,0:T(8,128)} %broadcast_in_dim.5), calls=%async_computation | async-start | bytes 524288 | tf_op jit(solution)/shard_map/all_to_all | solution.py:32
  127.6 0.0 all-gather.9.cloned.1.call-start
  128.3 0.0 copy-done.2
  128.4 9.0 %all-to-all-done = f32[8,8,1024]{2,1,0:T(8,128)S(1)} async-done(((f32[8,8,1024]{2,1,0:T(8,128)}), f32[8,8,1024]{2,1,0:T(8,128)S(1)}, u32[]{:S(2)}, u32[]{:S(2)}) %all-to-all-start) | async-done | bytes 262176 | tf_op jit(solution)/shard_map/all_to_all | solution.py:32
  137.4 4.5 %fusion.1 = bf16[8,2048]{1,0:T(8,128)(2,1)} fusion(bf16[2048,1024]{0,1:T(8,128)(2,1)} %bitcast.21, bf16[8,2048]{1,0:T(8,128)(2,1)S(1)} %copy-done.1, f32[]{:T(128)} %bitcast.19, f32[8,1024]{1,0:T(8,128)S(1)} %reduce_sum.9, f32[1024]{0:T(1024)S(1)} %add_divide_fusion), kind=kOutput, calls=%fused_computation.2 | convolution fusion | flops 201400320 | bytes 4296708 | tf_op jit(solution)/shard_map/dot_general | solution.py:52
  142.0 0.0 all-gather.9.cloned.1.call-update
  142.0 0.0 reduce-scatter.2.cloned.1.call-start
  142.0 134.0 %all-gather.9.cloned.1.call-done = bf16[512,2048]{1,0:T(8,128)(2,1)} async-done(((bf16[8,2048]{1,0:T(8,128)(2,1)}), bf16[512,2048]{1,0:T(8,128)(2,1)}) %all-gather.9.cloned.1.call-update) | async-done | bytes 2097168 | tf_op jit(solution)/shard_map/all_gather | solution.py:54
  276.1 6.5 %fusion.5 = f32[512,1024]{1,0:T(8,128)} fusion(bf16[512,2048]{1,0:T(8,128)(2,1)} %all-gather.9.cloned.1.call-done, bf16[1024,2048]{1,0:T(8,128)(2,1)} %param.9), kind=kOutput, calls=%fused_computation.8 | convolution fusion | flops 2147483648 | bytes 8388608 | tf_op jit(solution)/shard_map/qk,nk->qn/dot_general | solution.py:42
  282.6 0.0 reduce-scatter.2.cloned.1.call-update
  282.6 40.1 %reduce-scatter.2.cloned.1.call-done = f32[64,1024]{1,0:T(8,128)} async-done(((f32[512,1024]{1,0:T(8,128)}), f32[64,1024]{1,0:T(8,128)}) %reduce-scatter.2.cloned.1.call-update) | async-done | bytes 262160 | tf_op jit(solution)/shard_map/reduce_scatter | solution.py:55
  322.7 1.6 convert_element_type.12
  (2 shorter events, 0.0 us)
Async XLA Ops:
  6.5 57.8 %all-gather.5.cloned.1.call-start = ((), (), s32[]{:S(2)}) async-start(), calls=%async_computation.2 | async-start | bytes 1179648 | tf_op jit(solution)/shard_map/all_gather | solution.py:19
  16.9 99.5 %all-gather.7.cloned.1.call-start = ((), (), s32[]{:S(2)}) async-start(), calls=%async_computation.3 | async-start | bytes 5242880 | tf_op jit(solution)/shard_map/all_gather | solution.py:19
  116.4 4.5 %copy-start.1 = (bf16[8,2048]{1,0:T(8,128)(2,1)S(1)}, bf16[8,2048]{1,0:T(8,128)(2,1)}, u32[]{:S(2)}) copy-start(bf16[8,2048]{1,0:T(8,128)(2,1)} %param.5) | copy-start | bytes 98308
  118.9 2.0 copy-start
  118.9 9.4 %copy-start.2 = (f32[1024]{0:T(1024)S(1)}, f32[1024]{0:T(1024)}, u32[]{:S(2)}) copy-start(f32[1024]{0:T(1024)} %param.7) | copy-start | bytes 12292
  122.8 14.6 %all-to-all-start = ((f32[8,8,1024]{2,1,0:T(8,128)}), f32[8,8,1024]{2,1,0:T(8,128)S(1)}, u32[]{:S(2)}, u32[]{:S(2)}) async-start(f32[8,8,1024]{2,1,0:T(8,128)} %broadcast_in_dim.5), calls=%async_computation | async-start | bytes 524288 | tf_op jit(solution)/shard_map/all_to_all | solution.py:32
  127.6 148.4 %all-gather.9.cloned.1.call-start = ((), (), s32[]{:S(2)}) async-start(), calls=%async_computation.4 | async-start | bytes 2129920 | tf_op jit(solution)/shard_map/all_gather | solution.py:54
  142.0 180.7 %reduce-scatter.2.cloned.1.call-start = ((), (), s32[]{:S(2)}) async-start(), calls=%async_computation.5 | async-start | bytes 2359296 | tf_op jit(solution)/shard_map/reduce_scatter | solution.py:55
Sparse Core Ops, SparseCore 0:
  17.1 47.2 all-gather.4
  66.5 49.8 all-gather.6
  142.1 133.9 all-gather.8
  282.7 39.9 reduce-scatter.1
where the time goes:
time: 331 us
  waiting for transfers between devices  283 us (85%)
  between operations  13.8 us (4%)
  matrix products  12.2 us (4%)
  blocking collectives  9.7 us (3%)
  local copies, waits for them, and re-layouts  5.85 us (2%)
  starting transfers between devices  4.97 us (2%)
    all_gather x1, waiting for transfers between devices, per_device(): lax.all_gather(pre_own, BLK, axis=0, tiled=True)  134 us
    all_gather x2, waiting for transfers between devices, stacked_from(): tiles = lax.all_gather(tiles, axes[k], axis=0, tiled=True)  99.4 us
    reduce_scatter x1, waiting for transfers between devices, per_device(): lax.psum_scatter(partial_scores, 'col', scatter_dimension=0, tiled=True)  40.1 us
    all_gather x1, blocking collectives, stacked_from(): tiles = lax.all_gather(tiles, axes[k], axis=0, tiled=True)  9.7 us
    all_to_all x1, waiting for transfers between devices, from_everyone(): lax.all_to_all(jnp.broadcast_to(shard[None], (length, *shard.shape)), axi...  9.03 us
  transfers between devices with their start and end apart: 5, of which 5 were waited for; matrix products, arithmetic and copies ran while one was open for 0% of the time, Pallas kernels for 0%

commit v1 on v0

--- a/solution.py
+++ b/solution.py
@@ -51,7 +51,17 @@
     scaled = coefficient * weights[None, :]
     correction = jnp.dot(scaled, full_factor.astype(jnp.float32).T, precision=lax.Precision.HIGHEST)
     pre_own = ((queries.astype(jnp.float32) - correction) / damp_value).astype(jnp.bfloat16)
-    partial_scores = row_scores(lax.all_gather(pre_own, BLK, axis=0, tiled=True), train_rows)
+
+    def drive_the_quarters(block_in, across):
+        res = jnp.concatenate(
+            lax.all_to_all(
+                jnp.stack([block_in for _ in range(lax.axis_size(across))], axis=0), across, 0, 0
+            ),
+            axis=0,
+        )
+        return res
+
+    partial_scores = row_scores(drive_the_quarters(pre_own, BLK), train_rows)
     scores = lax.psum_scatter(partial_scores, "col", scatter_dimension=0, tiled=True)
     return scores.astype(jnp.bfloat16)
 

time: 331 us -> 261 us (0.79)
  waiting for transfers between devices: 283 us -> 147 us
  blocking collectives: 9.7 us -> 78 us
  matrix products: 12.2 us -> 8.81 us
    all_gather x1 -> x0, waiting for transfers between devices: 134 us -> none  [per_device(): lax.all_gather(pre_own, BLK, axis=0, tiled=True)]
    all_to_all x0 -> x1, blocking collectives: none -> 68.3 us  [drive_the_quarters(): lax.all_to_all(jnp.stack([block_in for _ in range(lax.axis_size(across))]...]
  transfers between devices with their start and end apart: 5 -> 4, of which waited for: 5 -> 4; matrix products, arithmetic and copies ran while one was open for 0% -> 0% of each run, Pallas kernels for 0% -> 0%
where the time goes in v1:
time: 261 us; the launch traced here: 260 us
  waiting for transfers between devices  147 us (56%)
  blocking collectives  78 us (30%)
  between operations  13.8 us (5%)
  matrix products  8.81 us (3%)
  local copies, waits for them, and re-layouts  6.09 us (2%)
  starting transfers between devices  4.92 us (2%)
    all_gather x2, waiting for transfers between devices, stacked_from(): tiles = lax.all_gather(tiles, axes[k], axis=0, tiled=True)  99.4 us
    all_to_all x1, blocking collectives, drive_the_quarters(): lax.all_to_all(jnp.stack([block_in for _ in range(lax.axis_size(across))]...  68.3 us
    reduce_scatter x1, waiting for transfers between devices, per_device(): lax.psum_scatter(partial_scores, 'col', scatter_dimension=0, tiled=True)  38.4 us
    all_gather x1, blocking collectives, stacked_from(): tiles = lax.all_gather(tiles, axes[k], axis=0, tiled=True)  9.7 us
    all_to_all x1, waiting for transfers between devices, from_everyone(): lax.all_to_all(jnp.broadcast_to(shard[None], (length, *shard.shape)), axi...  9.03 us
  transfers between devices with their start and end apart: 4, of which 4 were waited for; matrix products, arithmetic and copies ran while one was open for 0% of the time, Pallas kernels for 0%

profile of v1, /device:TPU:6, one launch (start us, length us, event | category | flops | bytes accessed | tf_op | source)
XLA Modules:
  0.0 260.2 jit_solution(1611831401315342287)
XLA Ops:
  6.5 0.0 all-gather.4.cloned.1.call-start
  6.5 9.7 %all-gather = bf16[4096,16]{0,1:T(8,128)(2,1)S(1)} all-gather(bf16[2048,16]{0,1:T(8,128)(2,1)} %param.6), channel_id=2, replica_groups=mesh['blk_0'=8,'blk_1'=2,'blk_2'=4,'col'=8] {'blk_1'}, dimensions={0}, use_global_device_ids=true | all-gather | bytes 196608 | tf_op jit(solution)/shard_map/all_gather | solution.py:19
  16.2 0.7 copy.17
  16.9 0.0 all-gather.4.cloned.1.call-update
  16.9 0.0 all-gather.6.cloned.1.call-start
  17.0 47.4 %all-gather.4.cloned.1.call-done = bf16[16,2048,16]{1,2,0:T(8,128)(2,1)} async-done(((bf16[2,2048,16]{1,2,0:T(8,128)(2,1)}), bf16[16,2048,16]{1,2,0:T(8,128)(2,1)}) %all-gather.4.cloned.1.call-update) | async-done | bytes 1048592 | tf_op jit(solution)/shard_map/all_gather | solution.py:19
  64.4 0.0 all-gather.6.cloned.1.call-update
  64.4 52.0 %all-gather.6.cloned.1.call-done = bf16[64,2048,16]{1,2,0:T(8,128)(2,1)} async-done(((bf16[16,2048,16]{1,2,0:T(8,128)(2,1)}), bf16[64,2048,16]{1,2,0:T(8,128)(2,1)}) %all-gather.6.cloned.1.call-update) | async-done | bytes 4194320 | tf_op jit(solution)/shard_map/all_gather | solution.py:19
  116.4 0.0 copy-start.1
  116.4 2.5 copy.14
  118.9 0.0 copy-start
  118.9 0.0 copy-start.2
  118.9 1.9 copy-done
  120.9 0.0 copy-done.1
  120.9 1.2 fusion.6
  122.1 0.7 broadcast_in_dim.5
  122.8 4.8 %all-to-all-start = ((f32[8,8,1024]{2,1,0:T(8,128)}), f32[8,8,1024]{2,1,0:T(8,128)S(1)}, u32[]{:S(2)}, u32[]{:S(2)}) async-start(f32[8,8,1024]{2,1,0:T(8,128)} %broadcast_in_dim.5), calls=%async_computation | async-start | bytes 524288 | tf_op jit(solution)/shard_map/all_to_all | solution.py:32
  127.6 0.0 reduce-scatter.2.cloned.1.call-start
  128.3 0.0 copy-done.2
  128.3 9.0 %all-to-all-done = f32[8,8,1024]{2,1,0:T(8,128)S(1)} async-done(((f32[8,8,1024]{2,1,0:T(8,128)}), f32[8,8,1024]{2,1,0:T(8,128)S(1)}, u32[]{:S(2)}, u32[]{:S(2)}) %all-to-all-start) | async-done | bytes 262176 | tf_op jit(solution)/shard_map/all_to_all | solution.py:32
  137.4 3.9 %fusion.1 = bf16[8,2048]{1,0:T(8,128)(2,1)S(1)} fusion(bf16[2048,1024]{0,1:T(8,128)(2,1)} %bitcast.23, bf16[8,2048]{1,0:T(8,128)(2,1)S(1)} %copy-done.1, f32[]{:T(128)} %bitcast.21, f32[8,1024]{1,0:T(8,128)S(1)} %reduce_sum.9, f32[1024]{0:T(1024)S(1)} %add_divide_fusion), kind=kOutput, calls=%fused_computation.2 | convolution fusion | flops 201400320 | bytes 4296708 | tf_op jit(solution)/shard_map/dot_general | solution.py:52
  141.3 0.0 copy-start.3
  141.3 0.2 stack.2
  141.6 68.3 %all_to_all.10 = bf16[64,8,2048]{2,1,0:T(8,128)(2,1)S(1)} all-to-all(bf16[64,8,2048]{2,1,0:T(8,128)(2,1)S(1)} %stack.2), channel_id=1, replica_groups=mesh['blk_0'=8,'blk_1'=2,'blk_2'=4,'col'=8] {'blk_0','blk_1','blk_2'}, dimensions={0} | all-to-all | bytes 4194304 | tf_op jit(solution)/shard_map/all_to_all | solution.py:57
  209.9 0.0 copy-done.3
  209.9 3.7 %fusion.2 = f32[512,1024]{1,0:T(8,128)} fusion(bf16[1024,2048]{1,0:T(8,128)(2,1)S(1)} %copy-done.3, bf16[64,8,2048]{2,1,0:T(8,128)(2,1)S(1)} %all_to_all.10), kind=kOutput, calls=%fused_computation.3 | convolution fusion | flops 2147483648 | bytes 8388608 | tf_op jit(solution)/shard_map/qk,nk->qn/dot_general | solution.py:42
  213.6 0.0 reduce-scatter.2.cloned.1.call-update
  213.6 38.4 %reduce-scatter.2.cloned.1.call-done = f32[64,1024]{1,0:T(8,128)} async-done(((f32[512,1024]{1,0:T(8,128)}), f32[64,1024]{1,0:T(8,128)}) %reduce-scatter.2.cloned.1.call-update) | async-done | bytes 262160 | tf_op jit(solution)/shard_map/reduce_scatter | solution.py:65
  252.0 1.6 convert_element_type.12
  (2 shorter events, 0.0 us)
Async XLA Ops:
  6.5 57.8 %all-gather.4.cloned.1.call-start = ((), (), s32[]{:S(2)}) async-start(), calls=%async_computation.3 | async-start | bytes 1179648 | tf_op jit(solution)/shard_map/all_gather | solution.py:19
  16.9 99.5 %all-gather.6.cloned.1.call-start = ((), (), s32[]{:S(2)}) async-start(), calls=%async_computation.4 | async-start | bytes 5242880 | tf_op jit(solution)/shard_map/all_gather | solution.py:19
  116.4 4.5 %copy-start.1 = (bf16[8,2048]{1,0:T(8,128)(2,1)S(1)}, bf16[8,2048]{1,0:T(8,128)(2,1)}, u32[]{:S(2)}) copy-start(bf16[8,2048]{1,0:T(8,128)(2,1)} %param.5) | copy-start | bytes 98308
  118.9 1.9 copy-start
  118.9 9.4 %copy-start.2 = (f32[1024]{0:T(1024)S(1)}, f32[1024]{0:T(1024)}, u32[]{:S(2)}) copy-start(f32[1024]{0:T(1024)} %param.7) | copy-start | bytes 12292
  122.8 14.6 %all-to-all-start = ((f32[8,8,1024]{2,1,0:T(8,128)}), f32[8,8,1024]{2,1,0:T(8,128)S(1)}, u32[]{:S(2)}, u32[]{:S(2)}) async-start(f32[8,8,1024]{2,1,0:T(8,128)} %broadcast_in_dim.5), calls=%async_computation | async-start | bytes 524288 | tf_op jit(solution)/shard_map/all_to_all | solution.py:32
  127.6 124.4 %reduce-scatter.2.cloned.1.call-start = ((), (), s32[]{:S(2)}) async-start(), calls=%async_computation.5 | async-start | bytes 2359296 | tf_op jit(solution)/shard_map/reduce_scatter | solution.py:65
  141.3 68.6 %copy-start.3 = (bf16[1024,2048]{1,0:T(8,128)(2,1)S(1)}, bf16[1024,2048]{1,0:T(8,128)(2,1)}, u32[]{:S(2)}) copy-start(bf16[1024,2048]{1,0:T(8,128)(2,1)} %param.9) | copy-start | bytes 12582916
Sparse Core Ops, SparseCore 0:
  17.1 47.2 all-gather.3
  66.5 49.8 all-gather.5
  213.7 38.2 reduce-scatter.1
